TPU v7x, 32 devices: a whole 2x2x4 slice. The times are simulated.
32 devices in a mesh: visit: 8 (over y, x, core), strip: 4 (over z).
Axes of the slice: x: 2, y: 2, z: 4, core: 2. Of those that a mesh axis runs over, the one named last changes fastest.
Arguments:
- warped: float32 [8, 256, 2048], P('visit', None, 'strip'), may hold values from -8 to 8
- variance: float32 [8, 256, 2048], P('visit', None, 'strip'), may hold values from 1 to 16
- bad_pixels: int32 [8, 256, 2048], P('visit', None, 'strip'), may hold values 0 or 1
- row_offset: int32 [8], P('visit'), may hold values from 0 to 255
- visit_group: int32 [8], P('visit'), may hold values from 0 to 1
- coefficient: float32 [8, 9, 3], P('visit'), may hold values from -3 to 3
- basis_rows: float32 [9, 21], replicated, may hold values from -1.2 to 1.2
- basis_cols: float32 [9, 21], replicated, may hold values from -1.2 to 1.2
Outputs:
- flux_sum: float32 [2, 256, 2048], P(None, 'strip', 'visit')
- weight_sum: float32 [2, 256, 2048], P(None, 'strip', 'visit')
All inputs are finite; a program needn't handle non-finite values. No bound on the sum of `bad_pixels` on one device may be relied on, other than what follows from the above.
Results may differ from a plain program's by a relative error of at most 0.0003.
Values sent between devices are 32-bit elements; how exact they have to be, the bound alone decides.
A program may use at most 64 MiB of HBM per device.

v0:
```python
import jax
import jax.numpy as jnp
from jax import lax
from jax.sharding import PartitionSpec as P

NGROUP = 2


def padded(x, sides, width):
    for axis, dim in sides:
        peers, length = (lax.axis_size(axis), x.shape[dim])
        up = [(i, (i + 1) % peers) for i in range(peers - 1)]
        down = [(j, i) for i, j in up]
        last = lax.slice_in_dim(x, length - width, length, axis=dim)
        leading = lax.slice_in_dim(x, 0, width, axis=dim)
        before = lax.ppermute(last, axis, up)
        after = lax.ppermute(leading, axis, down)
        x = jnp.concatenate([before, x, after], axis=dim)
    return x


def column_pass(image_rows, basis_cols, radius):
    vis, span, wide = image_rows.shape
    block = 128
    nblocks = wide // block
    blocks = image_rows.reshape(vis, span, nblocks, block)
    zeros = jnp.zeros((vis, span, 1, radius), jnp.float32)
    left = jnp.concatenate([zeros, blocks[:, :, :-1, block - radius :]], axis=2)
    right = jnp.concatenate([blocks[:, :, 1:, :radius], zeros], axis=2)
    windows = jnp.concatenate([left, blocks, right], axis=3)
    offsets = jnp.arange(block + 2 * radius)[:, None] - jnp.arange(block)[None, :]
    onehot = (offsets[:, :, None] == jnp.arange(2 * radius + 1)[None, None, :]).astype(jnp.float32)
    table = jnp.einsum("ioj,kj->kio", onehot, basis_cols, precision=lax.Precision.HIGHEST)
    filtered = jnp.einsum("vsni,kio->vksno", windows, table, precision=lax.Precision.HIGHEST)
    return filtered.reshape(vis, basis_cols.shape[0], span, wide)


def roll_rows(plane, shift):
    doubled = jnp.concatenate([plane, plane], axis=0)
    return lax.dynamic_slice_in_dim(doubled, shift, plane.shape[0], 0)


def on_device(
    warped, variance, bad_pixels, row_offset, visit_group, coefficient, basis_rows, basis_cols
):
    vis, total, narrow = warped.shape
    strips = lax.axis_size("strip")
    rows = total // strips
    radius = basis_rows.shape[1] // 2
    weight = (1.0 - bad_pixels.astype(jnp.float32)) / variance
    aligned = jax.vmap(roll_rows)(warped, row_offset)
    aligned_weight = jax.vmap(roll_rows)(weight, row_offset)
    image_strip, weight_rows = (
        lax.all_to_all(aligned, "strip", split_axis=1, concat_axis=2, tiled=True),
        lax.all_to_all(aligned_weight, "strip", split_axis=1, concat_axis=2, tiled=True),
    )
    image_rows = padded(image_strip, (("strip", 1),), radius)
    filtered = column_pass(image_rows, basis_cols, radius)
    span = rows + 2 * radius
    offsets = jnp.arange(span)[None, :] - jnp.arange(rows)[:, None]
    onehot = (offsets[:, :, None] == jnp.arange(2 * radius + 1)[None, None, :]).astype(jnp.float32)
    row_table = jnp.einsum("rsj,kj->krs", onehot, basis_rows, precision=lax.Precision.HIGHEST)
    first = lax.axis_index("strip") * rows
    height = rows * strips
    ypos = 2.0 * (first + jnp.arange(rows)).astype(jnp.float32) / (height - 1) - 1.0
    width_all = image_rows.shape[2]
    xpos = 2.0 * jnp.arange(width_all).astype(jnp.float32) / (width_all - 1) - 1.0
    leading = (
        coefficient[:, :, 0][:, :, None] + coefficient[:, :, 2][:, :, None] * ypos[None, None, :]
    )
    mixers = jnp.stack(
        [
            leading[:, :, :, None] * row_table[None],
            coefficient[:, :, 1][:, :, None, None] * row_table[None],
        ],
        axis=1,
    )
    terms = jnp.einsum("vjkrs,vksw->vjrw", mixers, filtered, precision=lax.Precision.HIGHEST)
    matched = terms[:, 0] + xpos[None, None, :] * terms[:, 1]
    member = (visit_group[:, None] == jnp.arange(NGROUP)[None, :]).astype(jnp.float32)
    flux_part = jnp.einsum(
        "vg,vrw->grw", member, weight_rows * matched, precision=lax.Precision.HIGHEST
    )
    weight_part = jnp.einsum("vg,vrw->grw", member, weight_rows, precision=lax.Precision.HIGHEST)
    flux_all, weight_all = lax.psum((flux_part, weight_part), "visit")
    piece = flux_all.shape[2] // lax.axis_size("visit")
    start = lax.axis_index("visit") * piece
    flux_sum = lax.dynamic_slice_in_dim(flux_all, start, piece, 2)
    weight_sum = lax.dynamic_slice_in_dim(weight_all, start, piece, 2)
    return (flux_sum, weight_sum)


def solution(mesh):
    return jax.shard_map(
        on_device,
        mesh=mesh,
        in_specs=(
            P("visit", None, "strip"),
            P("visit", None, "strip"),
            P("visit", None, "strip"),
            P("visit"),
            P("visit"),
            P("visit", None, None),
            P(),
            P(),
        ),
        out_specs=(P(None, "strip", "visit"), P(None, "strip", "visit")),
        check_vma=False,
    )
```

profile of v0, /device:TPU:0, one launch (start us, length us, event | category | flops | bytes accessed | tf_op | source)
XLA Modules:
  0.0 150.7 jit_solution(10829273639638241768)
XLA Ops:
  7.2 0.0 copy-start
  7.8 1.2 fusion.13
  9.1 0.0 copy-start.9
  9.1 0.0 copy-start.6
  9.1 0.0 copy-start.7
  9.1 1.3 copy.57
  10.4 6.3 %all-to-all-start.1 = ((f32[1,256,512]{2,0,1:T(1,128)}), f32[1,256,512]{2,0,1:T(1,128)S(1)}, u32[]{:S(2)}, u32[]{:S(2)}) async-start(f32[1,256,512]{2,0,1:T(1,128)} %copy.57), calls=%async_computation.1 | async-start | bytes 1048576 | tf_op jit(solution)/shard_map/all_to_all | solution.py:54
  16.8 0.1 multiply_add_fusion.1
  16.8 0.1 copy.42
  16.9 0.1 subtract_divide_fusion
  17.1 0.2 fusion.14
  17.3 0.0 copy-start.8
  17.3 1.4 copy.56
  18.7 1.8 %fusion.1 = f32[9,148,128,1]{2,0,1,3:T(8,128)} fusion(s32[148,128]{1,0:T(8,128)S(1)} %iota_subtract_fusion, f32[9,21]{1,0:T(8,128)S(1)} %copy-done), kind=kOutput, calls=%fused_computation.4 | convolution fusion | flops 43362816 | bytes 758516 | tf_op jit(solution)/shard_map/ioj,kj->kio/dot_general | solution.py:33
  20.5 0.4 multiply_bitcast_fusion.1
  20.9 10.4 %all-to-all-done.1 = f32[1,256,512]{2,0,1:T(1,128)S(1)} async-done(((f32[1,256,512]{2,0,1:T(1,128)}), f32[1,256,512]{2,0,1:T(1,128)S(1)}, u32[]{:S(2)}, u32[]{:S(2)}) %all-to-all-start.1) | async-done | bytes 524320 | tf_op jit(solution)/shard_map/all_to_all | solution.py:54
  31.3 3.5 %all-to-all-start = ((f32[1,256,512]{2,0,1:T(1,128)}), f32[1,256,512]{2,0,1:T(1,128)S(1)}, u32[]{:S(2)}, u32[]{:S(2)}) async-start(f32[1,256,512]{2,0,1:T(1,128)} %copy.56), calls=%async_computation | async-start | bytes 1048576 | tf_op jit(solution)/shard_map/all_to_all | solution.py:55
  34.8 0.0 all-reduce.5.cloned.1.call-start
  35.5 1.1 maximum_bitcast_fusion.2
  36.6 0.5 copy.44
  37.1 1.3 fusion.21
  38.4 1.5 %copy.58 = f32[1,10,2048]{2,0,1:T(1,128)S(1)} copy(f32[1,10,2048]{1,2,0:T(8,128)} %get-tuple-element.30) | data formatting | bytes 163840
  39.9 3.9 %collective-permute-start = (f32[1,10,2048]{2,0,1:T(1,128)S(1)}, f32[1,10,2048]{2,0,1:T(1,128)S(1)}, u32[]{:S(2)}, u32[]{:S(2)}) collective-permute-start(f32[1,10,2048]{2,0,1:T(1,128)S(1)} %copy.58), channel_id=1, source_target_pairs={{0,1},{1,2},{2,3},{4,5},{5,6},{6,7},{8,9},{9,10},{10,11},{12,13},{... | collective-permute-start | bytes 245768 | tf_op jit(solution)/shard_map/ppermute | solution.py:16
  43.8 0.3 copy.59
  44.1 1.5 collective-permute-start.1
  45.6 3.9 %all-to-all-done = f32[1,256,512]{2,0,1:T(1,128)S(1)} async-done(((f32[1,256,512]{2,0,1:T(1,128)}), f32[1,256,512]{2,0,1:T(1,128)S(1)}, u32[]{:S(2)}, u32[]{:S(2)}) %all-to-all-start) | async-done | bytes 524320 | tf_op jit(solution)/shard_map/all_to_all | solution.py:55
  49.5 0.3 copy.41
  49.8 1.0 copy.61
  50.8 0.4 copy.46
  51.1 0.0 collective-permute-done.1
  51.1 0.4 copy.47
  51.5 0.2 select_maximum_fusion.2
  51.7 1.1 copy-done.1
  52.8 6.9 %convolution_bitcast_fusion = f32[1,9,84,16,128]{4,2,3,1,0:T(8,128)S(1)} fusion(f32[1,84,16,10]{1,3,2,0:T(8,128)S(1)} %get-tuple-element.27, f32[1,10,16,128]{1,3,2,0:T(8,128)S(1)} %bitcast.75, f32[1,64,16,128]{1,3,2,0:T(8,128)S(1)} %bitcast.71, f32[1,10,16,128]{1,3,2,0:T(8,128)S(1)} %bitcast.73, f32[1,84,16,10]{1,3,2,0:T(8,128)S(1)} %get-tuple-element.26, ...), kind=kOutput, calls=%fused_computation | convolution fusion | flops 2750555136 | bytes 7670784 | tf_op jit(solution)/shard_map/vsni,kio->vksno/dot_general | solution.py:34
  59.7 3.7 %copy.49 = f32[1,9,84,16,128]{4,3,2,1,0:T(8,128)} copy(f32[1,9,84,16,128]{4,2,3,1,0:T(8,128)S(1)} %convolution_bitcast_fusion) | data formatting | bytes 12386304 | tf_op jit(solution)/shard_map/vsni,kio->vksno/transpose | solution.py:34
  63.3 6.9 %reshape.273 = f32[9,84,2048,1]{2,1,0,3:T(8,128)} reshape(f32[1,9,84,16,128]{4,3,2,1,0:T(8,128)} %copy.49) | data formatting | bytes 12386304 | tf_op jit(solution)/shard_map/reshape.13
  70.3 7.0 %convolution_bitcast_fusion.1 = f32[1,2,64,2048]{3,2,1,0:T(8,128)S(1)} fusion(f32[9,84,2048,1]{2,1,0,3:T(8,128)} %reshape.273, f32[2,9,64,84]{3,1,2,0:T(8,128)S(1)} %copy-done.4), kind=kOutput, calls=%fused_computation.1 | convolution fusion | flops 2378170368 | bytes 7628800 | tf_op jit(solution)/shard_map/vjkrs,vksw->vjrw/dot_general | solution.py:78
  77.3 0.1 fusion.20
  77.4 0.4 squeeze.6
  77.8 0.4 squeeze.7
  78.1 0.3 copy-done.3
  78.4 0.5 bitcast_multiply_fusion
  78.9 0.2 copy.60
  79.1 0.4 copy-done.5
  79.5 1.6 %broadcast_multiply_fusion = (f32[2,64,2048]{2,1,0:T(8,128)}, f32[2,64,2048]{2,1,0:T(8,128)}) fusion(f32[64,2048]{1,0:T(8,128)S(1)} %bitcast.80, f32[2]{0:T(128)S(1)} %fusion.18, f32[64,2048]{1,0:T(8,128)S(1)} %bitcast.81), kind=kLoop, calls=%fused_computation.27 | loop fusion | flops 524288 | bytes 3145736 | tf_op jit(solution)/shard_map/vg,vrw->grw/dot_general | solution.py:84
  81.1 0.0 all-reduce.5.cloned.1.call-update
  81.1 61.1 %all-reduce.5.cloned.1.call-done = (f32[2,64,2048]{2,1,0:T(8,128)}, f32[2,64,2048]{2,1,0:T(8,128)}) async-done(((f32[2,64,2048]{2,1,0:T(8,128)}, f32[2,64,2048]{2,1,0:T(8,128)}), (f32[2,64,2048]{2,1,0:T(8,128)}, f32[2,64,2048]{2,1,0:T(8,128)})) %all-reduce.5.cloned.1.call-update) | async-done | bytes 2097168 | tf_op jit(solution)/shard_map/psum | solution.py:85
  142.2 1.7 %constant_dynamic-slice_fusion = (f32[2,64,256]{2,1,0:T(8,128)}, f32[2,64,256]{2,1,0:T(8,128)}) fusion(f32[2,64,2048]{2,1,0:T(8,128)} %get-tuple-element.25, s32[]{:T(128)S(6)} %select_n.9, f32[2,64,2048]{2,1,0:T(8,128)} %get-tuple-element.24), kind=kLoop, calls=%fused_computation.46 | loop fusion | bytes 524292 | tf_op jit(solution)/shard_map/dynamic_slice | solution.py:89
  (19 shorter events, 0.1 us)
Async XLA Ops:
  7.2 11.5 %copy-start = (f32[9,21]{1,0:T(8,128)S(1)}, f32[9,21]{1,0:T(8,128)}, u32[]{:S(2)}) copy-start(f32[9,21]{1,0:T(8,128)} %param.15) | copy-start | bytes 2272
  9.1 7.7 %copy-start.9 = (f32[1,9,3]{1,0,2:T(1,128)S(1)}, f32[1,9,3]{1,0,2:T(1,128)}, u32[]{:S(2)}) copy-start(f32[1,9,3]{1,0,2:T(1,128)} %param.13) | copy-start | bytes 328
  9.1 7.9 %copy-start.6 = (f32[1,256,512]{2,1,0:T(8,128)S(1)}, f32[1,256,512]{2,1,0:T(8,128)}, u32[]{:S(2)}) copy-start(f32[1,256,512]{2,1,0:T(8,128)} %param.9) | copy-start | bytes 1572868
  9.1 7.8 %copy-start.7 = (s32[1,256,512]{2,1,0:T(8,128)S(1)}, s32[1,256,512]{2,1,0:T(8,128)}, u32[]{:S(2)}) copy-start(s32[1,256,512]{2,1,0:T(8,128)} %param.10) | copy-start | bytes 1572868
  10.4 20.9 %all-to-all-start.1 = ((f32[1,256,512]{2,0,1:T(1,128)}), f32[1,256,512]{2,0,1:T(1,128)S(1)}, u32[]{:S(2)}, u32[]{:S(2)}) async-start(f32[1,256,512]{2,0,1:T(1,128)} %copy.57), calls=%async_computation.1 | async-start | bytes 1048576 | tf_op jit(solution)/shard_map/all_to_all | solution.py:54
  17.3 3.2 %copy-start.8 = (f32[9,21]{1,0:T(8,128)S(1)}, f32[9,21]{1,0:T(8,128)}, u32[]{:S(2)}) copy-start(f32[9,21]{1,0:T(8,128)} %param.14) | copy-start | bytes 2272
  31.3 18.1 %all-to-all-start = ((f32[1,256,512]{2,0,1:T(1,128)}), f32[1,256,512]{2,0,1:T(1,128)S(1)}, u32[]{:S(2)}, u32[]{:S(2)}) async-start(f32[1,256,512]{2,0,1:T(1,128)} %copy.56), calls=%async_computation | async-start | bytes 1048576 | tf_op jit(solution)/shard_map/all_to_all | solution.py:55
  34.8 107.4 %all-reduce.5.cloned.1.call-start = ((), (), s32[]{:S(2)}) async-start(), calls=%async_computation.2 | async-start | bytes 4194304 | tf_op jit(solution)/shard_map/psum | solution.py:85
  39.9 10.9 %collective-permute-start = (f32[1,10,2048]{2,0,1:T(1,128)S(1)}, f32[1,10,2048]{2,0,1:T(1,128)S(1)}, u32[]{:S(2)}, u32[]{:S(2)}) collective-permute-start(f32[1,10,2048]{2,0,1:T(1,128)S(1)} %copy.58), channel_id=1, source_target_pairs={{0,1},{1,2},{2,3},{4,5},{5,6},{6,7},{8,9},{9,10},{10,11},{12,13},{... | collective-permute-start | bytes 245768 | tf_op jit(solution)/shard_map/ppermute | solution.py:16
  44.1 7.0 %collective-permute-start.1 = (f32[1,10,2048]{2,0,1:T(1,128)S(1)}, f32[1,10,2048]{2,0,1:T(1,128)S(1)}, u32[]{:S(2)}, u32[]{:S(2)}) collective-permute-start(f32[1,10,2048]{2,0,1:T(1,128)S(1)} %copy.59), channel_id=1, source_target_pairs={{1,0},{2,1},{3,2},{5,4},{6,5},{7,6},{9,8},{10,9},{11,10},{13,12},{... | collective-permute-start | bytes 245768 | tf_op jit(solution)/shard_map/ppermute | solution.py:17
  49.5 1.3 copy-start.2
  51.5 1.3 copy-start.1
  63.3 6.9 %copy-start.4 = (f32[2,9,64,84]{3,1,2,0:T(8,128)S(1)}, f32[2,9,64,84]{3,1,2,0:T(8,128)}, u32[]{:S(2)}) copy-start(f32[2,9,64,84]{3,1,2,0:T(8,128)} %maximum_bitcast_fusion.2) | copy-start | bytes 1161220
  77.4 1.0 copy-start.3
  78.4 1.0 copy-start.5
Sparse Core Ops, SparseCore 0:
  81.2 60.9 all-reduce.4
where the time goes:
time: 151 us
  waiting for transfers between devices  75.3 us (50%)
  local copies, waits for them, and re-layouts  23.4 us (15%)
  matrix products  16.2 us (11%)
  between operations  15.6 us (10%)
  starting transfers between devices  15.2 us (10%)
  other arithmetic  5 us (3%)
    psum x1, waiting for transfers between devices, on_device(): flux_all, weight_all = lax.psum((flux_part, weight_part), 'visit')  61.1 us
    all_to_all x1, waiting for transfers between devices, on_device(): lax.all_to_all(aligned, 'strip', split_axis=1, concat_axis=2, tiled=True)  10.4 us
    unnamed x26, local copies, waits for them, and re-layouts  7.5 us
    dot_general x1, matrix products, on_device(): jnp.einsum('vjkrs,vksw->vjrw', mixers, filtered, precision=lax.Precision....  7.04 us
    another operation x1, local copies, waits for them, and re-layouts  6.91 us
    dot_general x1, matrix products, column_pass(): jnp.einsum('vsni,kio->vksno', windows, table, precision=lax.Precision.HIG...  6.88 us
    all_to_all x1, starting transfers between devices, on_device(): lax.all_to_all(aligned, 'strip', split_axis=1, concat_axis=2, tiled=True)  6.32 us
    ppermute x1, starting transfers between devices, padded(): before = lax.ppermute(last, axis, up)  3.86 us
  transfers between devices with their start and end apart: 5, of which 3 were waited for; matrix products, arithmetic and copies ran while one was open for 7% of the time, Pallas kernels for 0%

commit v1 on v0

v1 whole, which is shorter than its diff:
```python
import functools
import jax
import jax.numpy as jnp
from jax import lax
from jax.experimental import pallas as pl
from jax.experimental.pallas import tpu as pltpu
from jax.sharding import PartitionSpec as P

NGROUP = 2
LANES = 128
EDGE = 64
TAIL = 8
MESH = pl.DeviceIdType.MESH


def split(x):
    hi = x.astype(jnp.bfloat16)
    lo = (x - hi.astype(jnp.float32)).astype(jnp.bfloat16)
    return hi, lo


def dot3(ahi, alo, bhi, blo):
    dot = functools.partial(jnp.dot, preferred_element_type=jnp.float32)
    return dot(ahi, bhi) + dot(ahi, blo) + dot(alo, bhi)


def kernel(
    nvisit, nstrip,
    img, var, bad, off, grp, coef, brow, bcol,
    fout, wout,
    halo, w2, p2, ahi, alo, base, chi, clo, mhi, mlo, fhi, flo,
    wsend, fsend, wrecv, frecv,
    halo_send, halo_recv, wsend_sem, fsend_sem, wrecv_sem, frecv_sem,
):
    height, narrow = img.shape
    nb, ks = brow.shape
    radius = ks // 2
    rows = height // nstrip
    piece = fout.shape[2]
    per = narrow // piece
    block = mhi.shape[0] // 2
    depth = mhi.shape[1] // nb
    pad = (depth - block) // 2
    tall = fhi.shape[0] // nb
    cols = fhi.shape[1]
    v = lax.axis_index("visit")
    s = lax.axis_index("strip")
    home = v // per
    slot = v % per

    barrier = pltpu.get_barrier_semaphore()

    def greet(vv, ss):
        @pl.when(jnp.logical_not((vv == v) & (ss == s)))
        def _():
            pl.semaphore_signal(barrier, inc=1, device_id=(vv, ss), device_id_type=MESH)

    for q in range(nstrip):
        for p in range(per):
            greet(per * s + p, q)
    for u in range(nvisit):
        greet(u, home)

    @pl.when(s > 0)
    def _():
        pl.semaphore_signal(barrier, inc=1, device_id=(v, s - 1), device_id_type=MESH)

    @pl.when(s < nstrip - 1)
    def _():
        pl.semaphore_signal(barrier, inc=1, device_id=(v, s + 1), device_id_type=MESH)

    back = lax.rem(height - off[0], height)
    weight = (1.0 - bad[...].astype(jnp.float32)) / var[...]
    w2[...] = pltpu.roll(weight, back, 0)
    group = jnp.full((TAIL, piece), grp[0], jnp.int32).astype(jnp.float32)
    for q in range(nstrip):
        part = w2[q * rows : (q + 1) * rows, :]
        for p in range(per):
            wsend[q, p, 0:rows, :] = part[:, p * piece : (p + 1) * piece]
            wsend[q, p, rows : rows + TAIL, :] = group

    greeted = per * nstrip + nvisit - 2 * (home == s).astype(jnp.int32)
    greeted = greeted + (s > 0).astype(jnp.int32) + (s < nstrip - 1).astype(jnp.int32)
    pl.semaphore_wait(barrier, greeted)

    def to_left():
        return pltpu.make_async_remote_copy(
            src_ref=img.at[:, pl.ds(0, LANES)], dst_ref=halo.at[1],
            send_sem=halo_send.at[0], recv_sem=halo_recv.at[1],
            device_id=(v, s - 1), device_id_type=MESH,
        )

    def to_right():
        return pltpu.make_async_remote_copy(
            src_ref=img.at[:, pl.ds(narrow - LANES, LANES)], dst_ref=halo.at[0],
            send_sem=halo_send.at[1], recv_sem=halo_recv.at[0],
            device_id=(v, s + 1), device_id_type=MESH,
        )

    @pl.when(s > 0)
    def _():
        to_left().start()

    @pl.when(s < nstrip - 1)
    def _():
        to_right().start()

    def remote(send, recv, send_sem, recv_sem, q, p):
        return pltpu.make_async_remote_copy(
            src_ref=send.at[q, p], dst_ref=recv.at[v],
            send_sem=send_sem.at[q, p], recv_sem=recv_sem.at[v],
            device_id=(per * s + p, q), device_id_type=MESH,
        )

    def ship(send, recv, send_sem, recv_sem, q, p):
        mine = (per * s + p == v) & (s == q)

        @pl.when(mine)
        def _():
            pltpu.make_async_copy(send.at[q, p], recv.at[v], recv_sem.at[v]).start()

        @pl.when(jnp.logical_not(mine))
        def _():
            remote(send, recv, send_sem, recv_sem, q, p).start()

    for q in range(nstrip):
        for p in range(per):
            ship(wsend, wrecv, wsend_sem, wrecv_sem, q, p)

    lane = lax.broadcasted_iota(jnp.int32, (nb, 2 * LANES), 1)
    flipped = jnp.zeros((nb, 2 * LANES), jnp.float32)
    turn = (radius - EDGE - (ks - 1)) % (2 * LANES)
    skew = turn % 8
    for j in range(ks):
        flipped = jnp.where(lane == ks - 1 - j + skew, bcol[:, j : j + 1], flipped)
    base[0:nb, 0 : 2 * LANES] = flipped
    for k in range(nb):
        spread = jnp.broadcast_to(base[k : k + 1, 0 : 2 * LANES], (2 * LANES, 2 * LANES))
        spread = pltpu.roll(spread, turn - skew, 1, stride=1, stride_axis=0)
        hi, lo = split(spread[:, 0:LANES])
        chi[:, k * LANES : (k + 1) * LANES] = hi
        clo[:, k * LANES : (k + 1) * LANES] = lo

    base[...] = jnp.zeros_like(base)
    slide = (pad - radius) % depth
    start = slide % 8
    base[0:nb, start : start + ks] = brow[...]

    def row_table(first):
        r = lax.broadcasted_iota(jnp.int32, (block, depth), 0)
        c = lax.broadcasted_iota(jnp.int32, (block, depth), 1)
        inside = jnp.abs(c - pad - r) <= radius
        ri = lax.broadcasted_iota(jnp.int32, (block, LANES), 0) + first
        ypos = 2.0 * ri.astype(jnp.float32) / (height - 1) - 1.0
        for k in range(nb):
            spread = jnp.broadcast_to(base[k : k + 1, :], (block, depth))
            spread = pltpu.roll(spread, slide - start, 1, stride=1, stride_axis=0)
            spread = jnp.where(inside, spread, 0.0)
            lead = coef[k, 0] + coef[k, 2] * ypos
            lead = jnp.concatenate([lead] * (depth // LANES), axis=1)
            hi, lo = split(lead * spread)
            mhi[0:block, k * depth : (k + 1) * depth] = hi
            mlo[0:block, k * depth : (k + 1) * depth] = lo
            hi, lo = split(coef[k, 1] * spread)
            mhi[block : 2 * block, k * depth : (k + 1) * depth] = hi
            mlo[block : 2 * block, k * depth : (k + 1) * depth] = lo

    if height == block:
        row_table(0)

    p2[:, EDGE : EDGE + narrow] = img[...]

    @pl.when(s == 0)
    def _():
        halo[0] = jnp.zeros((height, LANES), jnp.float32)

    @pl.when(s == nstrip - 1)
    def _():
        halo[1] = jnp.zeros((height, LANES), jnp.float32)

    @pl.when(s > 0)
    def _():
        to_right().wait_recv()

    @pl.when(s < nstrip - 1)
    def _():
        to_left().wait_recv()

    p2[:, 0:EDGE] = halo[0, :, LANES - EDGE : LANES]
    p2[:, EDGE + narrow : 2 * EDGE + narrow] = halo[1, :, 0:EDGE]
    hi, lo = split(pltpu.roll(p2[...], back, 0))
    ahi[...] = hi
    alo[...] = lo

    if pad:
        fhi[...] = jnp.zeros_like(fhi)
        flo[...] = jnp.zeros_like(flo)
    for cb in range(narrow // cols):
        for b in range(cols // LANES):
            at = cb * cols + b * LANES
            f = dot3(
                ahi[:, at : at + 2 * LANES], alo[:, at : at + 2 * LANES], chi[...], clo[...]
            )
            for k in range(nb):
                hi, lo = split(f[:, k * LANES : (k + 1) * LANES])
                fhi[k * tall + pad : k * tall + pad + height, b * LANES : (b + 1) * LANES] = hi
                flo[k * tall + pad : k * tall + pad + height, b * LANES : (b + 1) * LANES] = lo
        ci = lax.broadcasted_iota(jnp.int32, (rows, cols), 1) + (s * narrow + cb * cols)
        xpos = 2.0 * ci.astype(jnp.float32) / (narrow * nstrip - 1) - 1.0
        for rb in range(height // block):
            if height != block:
                row_table(rb * block)
                res = jnp.zeros((2 * block, cols), jnp.float32)
                for k in range(nb):
                    span = pl.ds(k * tall + rb * block, depth)
                    cut = pl.ds(k * depth, depth)
                    res = res + dot3(mhi[:, cut], mlo[:, cut], fhi[span, :], flo[span, :])
            else:
                res = dot3(mhi[...], mlo[...], fhi[...], flo[...])
            for t in range(block // rows):
                q = rb * (block // rows) + t
                matched = (
                    res[t * rows : (t + 1) * rows]
                    + xpos * res[block + t * rows : block + (t + 1) * rows]
                )
                for i in range(cols // piece):
                    p = cb * (cols // piece) + i
                    fsend[q, p] = (
                        wsend[q, p, 0:rows, :] * matched[:, i * piece : (i + 1) * piece]
                    )
                    ship(fsend, frecv, fsend_sem, frecv_sem, q, p)

    def total(send, recv, send_sem, recv_sem, out):
        sums = [jnp.zeros((rows, piece), jnp.float32) for _ in range(NGROUP)]
        for u in range(nvisit):
            pltpu.make_async_copy(recv.at[u], recv.at[u], recv_sem.at[u]).wait()
            label = wrecv[u, rows : rows + 1, :]
            value = recv[u, 0:rows, :]
            for g in range(NGROUP):
                sums[g] = sums[g] + jnp.where(label == g, value, 0.0)
        for g in range(NGROUP):
            out[g] = sums[g]

    total(wsend, wrecv, wsend_sem, wrecv_sem, wout)
    total(fsend, frecv, fsend_sem, frecv_sem, fout)

    for send, recv, send_sem, recv_sem in (
        (wsend, wrecv, wsend_sem, wrecv_sem),
        (fsend, frecv, fsend_sem, frecv_sem),
    ):
        for q in range(nstrip):
            for p in range(per):
                @pl.when(jnp.logical_not((per * s + p == v) & (s == q)))
                def _():
                    remote(send, recv, send_sem, recv_sem, q, p).wait_send()

    @pl.when(s > 0)
    def _():
        to_left().wait_send()

    @pl.when(s < nstrip - 1)
    def _():
        to_right().wait_send()


def on_device(nvisit, nstrip, warped, variance, bad, offset, group, coefficient, brow, bcol):
    _, height, narrow = warped.shape
    nb, ks = brow.shape
    rows = height // nstrip
    piece = narrow * nstrip // nvisit
    per = narrow // piece
    block = min(height, 256)
    pad = 0 if block == height else LANES
    depth = block + 2 * pad
    tall = height + 2 * pad
    cols = min(narrow, 256)
    vmem = pl.BlockSpec(memory_space=pltpu.VMEM)
    smem = pl.BlockSpec(memory_space=pltpu.SMEM)
    f32, bf16 = jnp.float32, jnp.bfloat16
    dma = pltpu.SemaphoreType.DMA
    out = jax.ShapeDtypeStruct((NGROUP, rows, piece), f32)
    return pl.pallas_call(
        functools.partial(kernel, nvisit, nstrip),
        out_shape=(out, out),
        in_specs=[vmem, vmem, vmem, smem, smem, smem, vmem, vmem],
        out_specs=(vmem, vmem),
        scratch_shapes=[
            pltpu.VMEM((2, height, LANES), f32),
            pltpu.VMEM((height, narrow), f32),
            pltpu.VMEM((height, narrow + 2 * EDGE), f32),
            pltpu.VMEM((height, narrow + 2 * EDGE), bf16),
            pltpu.VMEM((height, narrow + 2 * EDGE), bf16),
            pltpu.VMEM((16, depth), f32),
            pltpu.VMEM((2 * LANES, nb * LANES), bf16),
            pltpu.VMEM((2 * LANES, nb * LANES), bf16),
            pltpu.VMEM((2 * block, nb * depth), bf16),
            pltpu.VMEM((2 * block, nb * depth), bf16),
            pltpu.VMEM((nb * tall, cols), bf16),
            pltpu.VMEM((nb * tall, cols), bf16),
            pltpu.VMEM((nstrip, per, rows + TAIL, piece), f32),
            pltpu.VMEM((nstrip, per, rows, piece), f32),
            pltpu.VMEM((nvisit, rows + TAIL, piece), f32),
            pltpu.VMEM((nvisit, rows, piece), f32),
            dma((2,)),
            dma((2,)),
            dma((nstrip, per)),
            dma((nstrip, per)),
            dma((nvisit,)),
            dma((nvisit,)),
        ],
        compiler_params=pltpu.CompilerParams(
            collective_id=0, has_side_effects=True, vmem_limit_bytes=52 * 2**20
        ),
    )(
        warped[0], variance[0], bad[0], offset, group, coefficient[0], brow, bcol
    )


def solution(mesh):
    return jax.shard_map(
        functools.partial(on_device, mesh.shape["visit"], mesh.shape["strip"]),
        mesh=mesh,
        in_specs=(
            P("visit", None, "strip"),
            P("visit", None, "strip"),
            P("visit", None, "strip"),
            P("visit"),
            P("visit"),
            P("visit", None, None),
            P(),
            P(),
        ),
        out_specs=(P(None, "strip", "visit"), P(None, "strip", "visit")),
        check_vma=False,
    )
```

time: 151 us -> 42.7 us (0.28)
  the two profiles are of different devices: /device:TPU:0 before, /device:TPU:27 now
where the time goes in v1:
time: 42.7 us; the launch traced here: 42.4 us
  Pallas kernels  35.3 us (83%)
  local copies, waits for them, and re-layouts  5.13 us (12%)
  between operations  1.98 us (5%)
    pallas_call x1, Pallas kernels, on_device(): pl.pallas_call(functools.partial(kernel, nvisit, nstrip), out_shape=(out,...  35.3 us
    unnamed x14, local copies, waits for them, and re-layouts  5.03 us

profile of v1, /device:TPU:27, one launch (start us, length us, event | category | flops | bytes accessed | tf_op | source)
XLA Modules:
  0.0 42.4 jit_solution(12058255101752070594)
XLA Ops:
  1.3 0.0 copy-start.5
  1.9 0.0 copy-start.4
  2.0 0.0 copy-start.3
  2.0 0.0 copy-done.5
  2.0 0.1 copy.11
  2.1 0.6 %copy-done.4 = f32[9,21]{1,0:T(8,128)S(1)} copy-done((f32[9,21]{1,0:T(8,128)S(1)}, f32[9,21]{1,0:T(8,128)}, u32[]{:S(2)}) %copy-start.4) | copy-done | bytes 780
  2.6 0.0 copy-done.3
  2.7 0.0 copy-start
  2.7 1.0 %copy-done = f32[1,256,512]{2,1,0:T(8,128)S(1)} copy-done((f32[1,256,512]{2,1,0:T(8,128)S(1)}, f32[1,256,512]{2,1,0:T(8,128)}, u32[]{:S(2)}) %copy-start) | copy-done | bytes 524312
  3.7 0.0 copy-start.1
  3.7 1.0 %copy-done.1 = f32[1,256,512]{2,1,0:T(8,128)S(1)} copy-done((f32[1,256,512]{2,1,0:T(8,128)S(1)}, f32[1,256,512]{2,1,0:T(8,128)}, u32[]{:S(2)}) %copy-start.1) | copy-done | bytes 524312
  4.7 0.0 copy-start.2
  4.7 1.0 %copy-done.2 = s32[1,256,512]{2,1,0:T(8,128)S(1)} copy-done((s32[1,256,512]{2,1,0:T(8,128)S(1)}, s32[1,256,512]{2,1,0:T(8,128)}, u32[]{:S(2)}) %copy-start.2) | copy-done | bytes 524312
  5.8 35.3 %shard_map.95 = (f32[2,64,256]{2,1,0:T(8,128)S(1)}, f32[2,64,256]{2,1,0:T(8,128)S(1)}) custom-call(f32[256,512]{1,0:T(8,128)S(1)} %bitcast.4, f32[256,512]{1,0:T(8,128)S(1)} %bitcast.5, s32[256,512]{1,0:T(8,128)S(1)} %bitcast.6, s32[1]{0:T(128)S(6)} %copy.14.off, s32[1]{0:T(128)S(6)} %copy.15.grp, f32[9,3]{1,0:T(8,128)S(1)} %bitcast.7, ...), custom_call_target="tpu_custom_call" | custom-call | tf_op jit(solution)/shard_map/pallas_call | solution.py:282
  41.1 0.7 %copy.16 = f32[2,64,256]{2,1,0:T(8,128)} copy(f32[2,64,256]{2,1,0:T(8,128)S(1)} %get-tuple-element.4) | data formatting | bytes 262144
  41.7 0.7 %copy.17 = f32[2,64,256]{2,1,0:T(8,128)} copy(f32[2,64,256]{2,1,0:T(8,128)S(1)} %get-tuple-element.5) | data formatting | bytes 262144
Async XLA Ops:
  1.3 0.7 %copy-start.5 = (f32[1,9,3]{1,0,2:T(1,128)S(1)}, f32[1,9,3]{1,0,2:T(1,128)}, u32[]{:S(2)}) copy-start(f32[1,9,3]{1,0,2:T(1,128)} %param.13) | copy-start | bytes 328
  1.9 0.7 %copy-start.4 = (f32[9,21]{1,0:T(8,128)S(1)}, f32[9,21]{1,0:T(8,128)}, u32[]{:S(2)}) copy-start(f32[9,21]{1,0:T(8,128)} %bcol.1) | copy-start | bytes 2272
  2.0 0.7 %copy-start.3 = (f32[9,21]{1,0:T(8,128)S(1)}, f32[9,21]{1,0:T(8,128)}, u32[]{:S(2)}) copy-start(f32[9,21]{1,0:T(8,128)} %brow.1) | copy-start | bytes 2272
  2.7 1.0 %copy-start = (f32[1,256,512]{2,1,0:T(8,128)S(1)}, f32[1,256,512]{2,1,0:T(8,128)}, u32[]{:S(2)}) copy-start(f32[1,256,512]{2,1,0:T(8,128)} %param.8) | copy-start | bytes 1572868
  3.7 1.0 %copy-start.1 = (f32[1,256,512]{2,1,0:T(8,128)S(1)}, f32[1,256,512]{2,1,0:T(8,128)}, u32[]{:S(2)}) copy-start(f32[1,256,512]{2,1,0:T(8,128)} %param.9) | copy-start | bytes 1572868
  4.7 1.0 %copy-start.2 = (s32[1,256,512]{2,1,0:T(8,128)S(1)}, s32[1,256,512]{2,1,0:T(8,128)}, u32[]{:S(2)}) copy-start(s32[1,256,512]{2,1,0:T(8,128)} %param.10) | copy-start | bytes 1572868

commit v2 on v1

--- a/solution.py
+++ b/solution.py
@@ -28,9 +28,9 @@
     nvisit, nstrip,
     img, var, bad, off, grp, coef, brow, bcol,
     fout, wout,
-    halo, w2, p2, ahi, alo, base, chi, clo, mhi, mlo, fhi, flo,
+    varv, badv, hsend, hrecv, w2, p2, ahi, alo, base, chi, clo, mhi, mlo, fhi, flo,
     wsend, fsend, wrecv, frecv,
-    halo_send, halo_recv, wsend_sem, fsend_sem, wrecv_sem, frecv_sem,
+    load_sem, halo_send, halo_recv, wsend_sem, fsend_sem, wrecv_sem, frecv_sem,
 ):
     height, narrow = img.shape
     nb, ks = brow.shape
@@ -48,6 +48,14 @@
     home = v // per
     slot = v % per
 
+    loads = [
+        pltpu.make_async_copy(var, varv, load_sem.at[0]),
+        pltpu.make_async_copy(bad, badv, load_sem.at[1]),
+        pltpu.make_async_copy(img, p2.at[:, pl.ds(LANES, narrow)], load_sem.at[2]),
+    ]
+    for load in loads:
+        load.start()
+
     barrier = pltpu.get_barrier_semaphore()
 
     def greet(vv, ss):
@@ -70,7 +78,9 @@
         pl.semaphore_signal(barrier, inc=1, device_id=(v, s + 1), device_id_type=MESH)
 
     back = lax.rem(height - off[0], height)
-    weight = (1.0 - bad[...].astype(jnp.float32)) / var[...]
+    loads[0].wait()
+    loads[1].wait()
+    weight = (1.0 - badv[...].astype(jnp.float32)) / varv[...]
     w2[...] = pltpu.roll(weight, back, 0)
     group = jnp.full((TAIL, piece), grp[0], jnp.int32).astype(jnp.float32)
     for q in range(nstrip):
@@ -79,53 +89,16 @@
             wsend[q, p, 0:rows, :] = part[:, p * piece : (p + 1) * piece]
             wsend[q, p, rows : rows + TAIL, :] = group
 
-    greeted = per * nstrip + nvisit - 2 * (home == s).astype(jnp.int32)
-    greeted = greeted + (s > 0).astype(jnp.int32) + (s < nstrip - 1).astype(jnp.int32)
-    pl.semaphore_wait(barrier, greeted)
-
-    def to_left():
-        return pltpu.make_async_remote_copy(
-            src_ref=img.at[:, pl.ds(0, LANES)], dst_ref=halo.at[1],
-            send_sem=halo_send.at[0], recv_sem=halo_recv.at[1],
-            device_id=(v, s - 1), device_id_type=MESH,
-        )
-
-    def to_right():
-        return pltpu.make_async_remote_copy(
-            src_ref=img.at[:, pl.ds(narrow - LANES, LANES)], dst_ref=halo.at[0],
-            send_sem=halo_send.at[1], recv_sem=halo_recv.at[0],
-            device_id=(v, s + 1), device_id_type=MESH,
-        )
-
-    @pl.when(s > 0)
-    def _():
-        to_left().start()
-
-    @pl.when(s < nstrip - 1)
-    def _():
-        to_right().start()
-
-    def remote(send, recv, send_sem, recv_sem, q, p):
-        return pltpu.make_async_remote_copy(
-            src_ref=send.at[q, p], dst_ref=recv.at[v],
-            send_sem=send_sem.at[q, p], recv_sem=recv_sem.at[v],
-            device_id=(per * s + p, q), device_id_type=MESH,
-        )
-
-    def ship(send, recv, send_sem, recv_sem, q, p):
-        mine = (per * s + p == v) & (s == q)
-
-        @pl.when(mine)
-        def _():
-            pltpu.make_async_copy(send.at[q, p], recv.at[v], recv_sem.at[v]).start()
-
-        @pl.when(jnp.logical_not(mine))
-        def _():
-            remote(send, recv, send_sem, recv_sem, q, p).start()
-
-    for q in range(nstrip):
-        for p in range(per):
-            ship(wsend, wrecv, wsend_sem, wrecv_sem, q, p)
+    loads[2].wait()
+    thin = LANES // 8
+    short = height // 8
+    for b in range(8):
+        span = slice(b * short, (b + 1) * short)
+        lanes = slice(b * thin, (b + 1) * thin)
+        hsend[0, :, lanes] = p2[span, LANES : LANES + thin]
+        hsend[1, :, lanes] = p2[span, LANES + narrow - thin : LANES + narrow]
+    p2[:, 0:LANES] = jnp.zeros((height, LANES), jnp.float32)
+    p2[:, LANES + narrow :] = jnp.zeros((height, LANES), jnp.float32)
 
     lane = lax.broadcasted_iota(jnp.int32, (nb, 2 * LANES), 1)
     flipped = jnp.zeros((nb, 2 * LANES), jnp.float32)
@@ -156,39 +129,83 @@
             spread = jnp.broadcast_to(base[k : k + 1, :], (block, depth))
             spread = pltpu.roll(spread, slide - start, 1, stride=1, stride_axis=0)
             spread = jnp.where(inside, spread, 0.0)
-            lead = coef[k, 0] + coef[k, 2] * ypos
+            lead = coef[0, 0, k] + coef[2, 0, k] * ypos
             lead = jnp.concatenate([lead] * (depth // LANES), axis=1)
             hi, lo = split(lead * spread)
             mhi[0:block, k * depth : (k + 1) * depth] = hi
             mlo[0:block, k * depth : (k + 1) * depth] = lo
-            hi, lo = split(coef[k, 1] * spread)
+            hi, lo = split(coef[1, 0, k] * spread)
             mhi[block : 2 * block, k * depth : (k + 1) * depth] = hi
             mlo[block : 2 * block, k * depth : (k + 1) * depth] = lo
 
     if height == block:
         row_table(0)
 
-    p2[:, EDGE : EDGE + narrow] = img[...]
-
-    @pl.when(s == 0)
-    def _():
-        halo[0] = jnp.zeros((height, LANES), jnp.float32)
-
-    @pl.when(s == nstrip - 1)
-    def _():
-        halo[1] = jnp.zeros((height, LANES), jnp.float32)
+    greeted = per * nstrip + nvisit - 2 * (home == s).astype(jnp.int32)
+    greeted = greeted + (s > 0).astype(jnp.int32) + (s < nstrip - 1).astype(jnp.int32)
+    pl.semaphore_wait(barrier, greeted)
+
+    def to_left():
+        return pltpu.make_async_remote_copy(
+            src_ref=hsend.at[0], dst_ref=hrecv.at[1],
+            send_sem=halo_send.at[0], recv_sem=halo_recv.at[1],
+            device_id=(v, s - 1), device_id_type=MESH,
+        )
+
+    def to_right():
+        return pltpu.make_async_remote_copy(
+            src_ref=hsend.at[1], dst_ref=hrecv.at[0],
+            send_sem=halo_send.at[1], recv_sem=halo_recv.at[0],
+            device_id=(v, s + 1), device_id_type=MESH,
+        )
 
     @pl.when(s > 0)
     def _():
+        to_left().start()
+
+    @pl.when(s < nstrip - 1)
+    def _():
+        to_right().start()
+
+    def remote(send, recv, send_sem, recv_sem, q, p):
+        return pltpu.make_async_remote_copy(
+            src_ref=send.at[q, p], dst_ref=recv.at[v],
+            send_sem=send_sem.at[q, p], recv_sem=recv_sem.at[v],
+            device_id=(per * s + p, q), device_id_type=MESH,
+        )
+
+    def ship(send, recv, send_sem, recv_sem, q, p):
+        mine = (per * s + p == v) & (s == q)
+
+        @pl.when(mine)
+        def _():
+            pltpu.make_async_copy(send.at[q, p], recv.at[v], recv_sem.at[v]).start()
+
+        @pl.when(jnp.logical_not(mine))
+        def _():
+            remote(send, recv, send_sem, recv_sem, q, p).start()
+
+    for t in range(nstrip):
+        for p in range(per):
+            ship(wsend, wrecv, wsend_sem, wrecv_sem, (s + v // 2 + t) % nstrip, p)
+
+
+    @pl.when(s > 0)
+    def _():
         to_right().wait_recv()
+        for b in range(8):
+            span = slice(b * short, (b + 1) * short)
+            p2[span, LANES - thin : LANES] = hrecv[0, :, b * thin : (b + 1) * thin]
 
     @pl.when(s < nstrip - 1)
     def _():
         to_left().wait_recv()
-
-    p2[:, 0:EDGE] = halo[0, :, LANES - EDGE : LANES]
-    p2[:, EDGE + narrow : 2 * EDGE + narrow] = halo[1, :, 0:EDGE]
-    hi, lo = split(pltpu.roll(p2[...], back, 0))
+        for b in range(8):
+            span = slice(b * short, (b + 1) * short)
+            p2[span, LANES + narrow : LANES + narrow + thin] = hrecv[1, :, b * thin : (b + 1) * thin]
+
+    aligned = pltpu.roll(p2[...], back, 0)
+    hi, lo = split(aligned[:, LANES - EDGE : LANES + narrow + EDGE])
     ahi[...] = hi
     alo[...] = lo
 
@@ -228,7 +245,11 @@
                     fsend[q, p] = (
                         wsend[q, p, 0:rows, :] * matched[:, i * piece : (i + 1) * piece]
                     )
-                    ship(fsend, frecv, fsend_sem, frecv_sem, q, p)
+
+        for t in range(nstrip):
+            for i in range(cols // piece):
+                p = cb * (cols // piece) + i
+                ship(fsend, frecv, fsend_sem, frecv_sem, (s + v // 2 + t) % nstrip, p)
 
     def total(send, recv, send_sem, recv_sem, out):
         sums = [jnp.zeros((rows, piece), jnp.float32) for _ in range(NGROUP)]
@@ -275,6 +296,7 @@
     tall = height + 2 * pad
     cols = min(narrow, 256)
     vmem = pl.BlockSpec(memory_space=pltpu.VMEM)
+    hbm = pl.BlockSpec(memory_space=pltpu.HBM)
     smem = pl.BlockSpec(memory_space=pltpu.SMEM)
     f32, bf16 = jnp.float32, jnp.bfloat16
     dma = pltpu.SemaphoreType.DMA
@@ -282,12 +304,15 @@
     return pl.pallas_call(
         functools.partial(kernel, nvisit, nstrip),
         out_shape=(out, out),
-        in_specs=[vmem, vmem, vmem, smem, smem, smem, vmem, vmem],
+        in_specs=[hbm, hbm, hbm, smem, smem, smem, vmem, vmem],
         out_specs=(vmem, vmem),
         scratch_shapes=[
-            pltpu.VMEM((2, height, LANES), f32),
             pltpu.VMEM((height, narrow), f32),
-            pltpu.VMEM((height, narrow + 2 * EDGE), f32),
+            pltpu.VMEM((height, narrow), jnp.int32),
+            pltpu.VMEM((2, height // 8, LANES), f32),
+            pltpu.VMEM((2, height // 8, LANES), f32),
+            pltpu.VMEM((height, narrow), f32),
+            pltpu.VMEM((height, narrow + 2 * LANES), f32),
             pltpu.VMEM((height, narrow + 2 * EDGE), bf16),
             pltpu.VMEM((height, narrow + 2 * EDGE), bf16),
             pltpu.VMEM((16, depth), f32),
@@ -301,6 +326,7 @@
             pltpu.VMEM((nstrip, per, rows, piece), f32),
             pltpu.VMEM((nvisit, rows + TAIL, piece), f32),
             pltpu.VMEM((nvisit, rows, piece), f32),
+            dma((3,)),
             dma((2,)),
             dma((2,)),
             dma((nstrip, per)),
@@ -309,10 +335,10 @@
             dma((nvisit,)),
         ],
         compiler_params=pltpu.CompilerParams(
-            collective_id=0, has_side_effects=True, vmem_limit_bytes=52 * 2**20
+            collective_id=0, has_side_effects=True, vmem_limit_bytes=64 * 2**20 - 510 * 2**10
         ),
     )(
-        warped[0], variance[0], bad[0], offset, group, coefficient[0], brow, bcol
+        warped[0], variance[0], bad[0], offset, group, jnp.transpose(coefficient, (2, 0, 1)), brow, bcol
     )
 
 

time: 42.7 us -> 37.6 us (0.88)
  the two profiles are of different devices: /device:TPU:27 before, /device:TPU:19 now
where the time goes in v2:
time: 37.6 us; the launch traced here: 37 us
  Pallas kernels  32.8 us (87%)
  local copies, waits for them, and re-layouts  2.26 us (6%)
  between operations  1.94 us (5%)
    pallas_call x1, Pallas kernels, on_device(): pl.pallas_call(functools.partial(kernel, nvisit, nstrip), out_shape=(out,...  32.8 us
    unnamed x4, local copies, waits for them, and re-layouts  2.26 us

profile of v2, /device:TPU:19, one launch (start us, length us, event | category | flops | bytes accessed | tf_op | source)
XLA Modules:
  0.0 37.0 jit_solution(6710459789219984476)
XLA Ops:
  1.9 32.8 %shard_map.95 = (f32[2,64,256]{2,1,0:T(8,128)}, f32[2,64,256]{2,1,0:T(8,128)}) custom-call(f32[256,512]{1,0:T(8,128)} %bitcast.4, f32[256,512]{1,0:T(8,128)} %bitcast.5, s32[256,512]{1,0:T(8,128)} %bitcast.6, s32[1]{0:T(128)S(6)} %copy.12.off, s32[1]{0:T(128)S(6)} %copy.13.grp, f32[3,1,9]{2,1,0:T(1,128)} %bitcast.7, f32[9,21]{1,0:T(8,128)} %brow.1, f32[9,21]{1,0:T(8,128)} %bcol.1), custom_call_target="tpu_custom_call" | custom-call | tf_op jit(solution)/shard_map/pallas_call | solution.py:304
  34.8 0.0 copy-start
  34.8 1.6 %copy.14 = f32[2,64,256]{2,1,0:T(8,128)} copy(f32[2,64,256]{2,1,0:T(8,128)} %get-tuple-element.4) | data formatting | bytes 262144
  36.4 0.0 copy-done
  36.4 0.7 %copy.15 = f32[2,64,256]{2,1,0:T(8,128)} copy(f32[2,64,256]{2,1,0:T(8,128)S(1)} %copy-done) | data formatting | bytes 262144
Async XLA Ops:
  34.8 1.6 %copy-start = (f32[2,64,256]{2,1,0:T(8,128)S(1)}, f32[2,64,256]{2,1,0:T(8,128)}, u32[]{:S(2)}) copy-start(f32[2,64,256]{2,1,0:T(8,128)} %get-tuple-element.5) | copy-start | bytes 393220

commit v3 on v2

--- a/solution.py
+++ b/solution.py
@@ -187,7 +187,7 @@
 
     for t in range(nstrip):
         for p in range(per):
-            ship(wsend, wrecv, wsend_sem, wrecv_sem, (s + v // 2 + t) % nstrip, p)
+            ship(wsend, wrecv, wsend_sem, wrecv_sem, (s + nstrip // 2 + t) % nstrip, p)
 
 
     @pl.when(s > 0)
@@ -249,7 +249,7 @@
         for t in range(nstrip):
             for i in range(cols // piece):
                 p = cb * (cols // piece) + i
-                ship(fsend, frecv, fsend_sem, frecv_sem, (s + v // 2 + t) % nstrip, p)
+                ship(fsend, frecv, fsend_sem, frecv_sem, (s + nstrip // 2 + t) % nstrip, p)
 
     def total(send, recv, send_sem, recv_sem, out):
         sums = [jnp.zeros((rows, piece), jnp.float32) for _ in range(NGROUP)]

time: 37.6 us -> 37.9 us (level)
  Pallas kernels: 32.8 us -> 33.5 us
    pallas_call x1, Pallas kernels: 32.8 us -> 33.5 us  [on_device(): pl.pallas_call(functools.partial(kernel, nvisit, nstrip), out_shape=(out,...]
where the time goes in v3:
time: 37.9 us; the launch traced here: 37.7 us
  Pallas kernels  33.5 us (88%)
  local copies, waits for them, and re-layouts  2.26 us (6%)
  between operations  1.94 us (5%)
    pallas_call x1, Pallas kernels, on_device(): pl.pallas_call(functools.partial(kernel, nvisit, nstrip), out_shape=(out,...  33.5 us
    unnamed x4, local copies, waits for them, and re-layouts  2.26 us

profile of v3, /device:TPU:19, one launch (start us, length us, event | category | flops | bytes accessed | tf_op | source)
XLA Modules:
  0.0 37.7 jit_solution(6651937529159650990)
XLA Ops:
  1.9 33.5 %shard_map.95 = (f32[2,64,256]{2,1,0:T(8,128)}, f32[2,64,256]{2,1,0:T(8,128)}) custom-call(f32[256,512]{1,0:T(8,128)} %bitcast.4, f32[256,512]{1,0:T(8,128)} %bitcast.5, s32[256,512]{1,0:T(8,128)} %bitcast.6, s32[1]{0:T(128)S(6)} %copy.12.off, s32[1]{0:T(128)S(6)} %copy.13.grp, f32[3,1,9]{2,1,0:T(1,128)} %bitcast.7, f32[9,21]{1,0:T(8,128)} %brow.1, f32[9,21]{1,0:T(8,128)} %bcol.1), custom_call_target="tpu_custom_call" | custom-call | tf_op jit(solution)/shard_map/pallas_call | solution.py:304
  35.4 0.0 copy-start
  35.4 1.6 %copy.14 = f32[2,64,256]{2,1,0:T(8,128)} copy(f32[2,64,256]{2,1,0:T(8,128)} %get-tuple-element.4) | data formatting | bytes 262144
  37.0 0.0 copy-done
  37.0 0.7 %copy.15 = f32[2,64,256]{2,1,0:T(8,128)} copy(f32[2,64,256]{2,1,0:T(8,128)S(1)} %copy-done) | data formatting | bytes 262144
Async XLA Ops:
  35.4 1.6 %copy-start = (f32[2,64,256]{2,1,0:T(8,128)S(1)}, f32[2,64,256]{2,1,0:T(8,128)}, u32[]{:S(2)}) copy-start(f32[2,64,256]{2,1,0:T(8,128)} %get-tuple-element.5) | copy-start | bytes 393220
